TPU v7x, 256 devices: a whole 4x4x8 slice. The times are simulated.
256 devices in a mesh: grp: 16 (over y, x_lo, core), slab: 16 (over z, x_hi).
Axes of the slice: x: 4 (x_hi: 2, x_lo: 2; x = x_hi * 2 + x_lo), y: 4, z: 8, core: 2. Of those that a mesh axis runs over, the one named last changes fastest.
Arguments:
- basis_atom_masses: bfloat16 [3, 256, 128, 128], P(None, 'slab'), may hold values from 0.03 to 34
- right_dual_factors: float32 [16, 3, 256, 128, 128], P('grp', None, 'slab'), may hold values from 0.03 to 34
- observed_mass_snapshot: float32 [16, 256, 128, 128], P('grp', 'slab'), may hold values from 0.03 to 34
- mixing_coefficient_tags: int32 [16, 3], P('grp'), may hold values from 1 to 16
Outputs:
- barycenter: float32 [16, 256, 128, 128], P('grp', 'slab')
- new_scalings: float32 [16, 3, 256, 128, 128], P('grp', None, 'slab')
- atom_gradient: float32 [3, 256, 128, 128], P(None, 'grp', 'slab')
All inputs are finite; a program needn't handle non-finite values.
Results may differ from a plain program's by a relative error of at most 0.0003.
Values may be sent and summed in bfloat16 or wider, within the bound.
A program may use at most 64 MiB of HBM per device.

v0:
```python
import math

import jax
import jax.numpy as jnp
from jax import lax
from jax.sharding import PartitionSpec as P

NX = 256
NY = 128
NZ = 128
REACH = 4


sharpness = 3.0


def profile(offset):
    values = jnp.exp(-sharpness * (offset / REACH) ** 2) / (REACH * math.sqrt(math.pi / sharpness))
    return jnp.where(jnp.abs(offset) <= REACH, values, jnp.zeros_like(values))


def gaussian(count):
    positions = jnp.arange(count)
    offset = (positions[:, None] - positions[None, :]).astype(jnp.float32)
    return profile(offset)


def local(basis_atom_masses, right_dual_factors, observed_mass_snapshot, mixing_coefficient_tags):
    highest = lax.Precision.HIGHEST
    abscissa_axis = gaussian(NX)
    ordinate_axis = gaussian(NY)
    height_axis = gaussian(NZ)
    right_dual_factor = right_dual_factors[0]
    goal_mass = observed_mass_snapshot[0]
    coefficient_line = mixing_coefficient_tags[0]
    blend = coefficient_line.astype(jnp.float32) / jnp.sum(coefficient_line).astype(jnp.float32)
    blend = blend[:, None, None, None]

    def sheets_axis_span(values):
        values = jnp.einsum("axyz,zw->axyw", values, height_axis, precision=highest)
        return jnp.einsum("axyz,yw->axwz", values, ordinate_axis, precision=highest)

    def across(values):
        return jnp.einsum("axyz,xw->awyz", values, abscissa_axis, precision=highest)

    def stacked_entries(values):
        return across(lax.all_to_all(values, "slab", split_axis=2, concat_axis=1, tiled=True))

    def reverse_lines(values):
        return lax.all_to_all(values, "slab", split_axis=1, concat_axis=2, tiled=True)

    blurred_right_factor = reverse_lines(stacked_entries(sheets_axis_span(right_dual_factor)))
    first_scale = basis_atom_masses.astype(jnp.float32) / blurred_right_factor
    kern_u = reverse_lines(stacked_entries(sheets_axis_span(first_scale)))
    barycenter = jnp.exp(jnp.sum(blend * jnp.log(kern_u), axis=0))
    new_scaling = barycenter[None] / kern_u
    pulled = blend * ((barycenter - goal_mass) * barycenter)[None] / kern_u
    gradient_planes = (
        reverse_lines(stacked_entries(sheets_axis_span(pulled))) / blurred_right_factor
    )
    gradient_cols = lax.all_to_all(gradient_planes, "slab", split_axis=2, concat_axis=1, tiled=True)
    sensitivity_mass = lax.psum_scatter(gradient_cols, "grp", scatter_dimension=1, tiled=True)
    return (barycenter[None], new_scaling[None], sensitivity_mass)


def solution(mesh):
    placed = (
        P(None, "slab", None, None),
        P("grp", None, "slab", None, None),
        P("grp", "slab", None, None),
        P("grp", None),
    )
    return jax.shard_map(
        local,
        mesh=mesh,
        in_specs=placed,
        out_specs=(
            P("grp", "slab", None, None),
            P("grp", None, "slab", None, None),
            P(None, "grp", "slab", None),
        ),
        check_vma=False,
    )
```

profile of v0, /device:TPU:30, one launch (start us, length us, event | category | flops | bytes accessed | tf_op | source)
XLA Modules:
  0.0 685.5 jit_solution(9106853549845797112)
XLA Ops:
  7.2 0.0 copy-start
  7.2 1.9 copy-done
  9.1 2.9 fusion.3
  12.0 2.8 fusion.9
  14.8 1.8 copy.99
  16.7 82.9 %all_to_all.129 = f32[3,16,128,128]{3,1,0,2:T(8,128)S(1)} all-to-all(f32[3,16,128,128]{3,1,0,2:T(8,128)S(1)} %copy.99), channel_id=1, replica_groups=mesh['grp'=16,'slab'=16] {'slab'}, dimensions={2} | all-to-all | bytes 6291456 | tf_op jit(solution)/shard_map/all_to_all | solution.py:47
  99.6 0.4 copy.100
  100.0 2.9 convolution_bitcast_fusion.4
  102.9 1.8 copy.101
  104.7 78.9 %all_to_all.130 = f32[3,256,8,128]{3,2,0,1:T(8,128)S(1)} all-to-all(f32[3,256,8,128]{3,2,0,1:T(8,128)S(1)} %copy.101), channel_id=1, replica_groups=mesh['grp'=16,'slab'=16] {'slab'}, dimensions={1} | all-to-all | bytes 6291456 | tf_op jit(solution)/shard_map/all_to_all | solution.py:50
  183.6 0.0 copy-start.6
  183.6 0.5 copy.102
  184.2 0.9 copy-done.6
  185.0 0.0 copy-start.3
  185.0 1.1 bitcast_divide_fusion.4
  186.1 0.6 copy-done.3
  186.7 3.4 fusion.5
  190.2 2.9 convolution_bitcast_fusion.1
  193.0 1.8 copy.105
  194.9 78.1 %all_to_all.131 = f32[3,16,128,128]{3,1,0,2:T(8,128)S(1)} all-to-all(f32[3,16,128,128]{3,1,0,2:T(8,128)S(1)} %copy.105), channel_id=1, replica_groups=mesh['grp'=16,'slab'=16] {'slab'}, dimensions={2} | all-to-all | bytes 6291456 | tf_op jit(solution)/shard_map/all_to_all | solution.py:47
  273.0 0.4 copy.106
  273.4 2.9 convolution_bitcast_fusion.3
  276.3 3.5 copy.107
  279.8 0.0 copy-start.8
  279.8 6.7 all-to-all-start.3
  286.5 0.0 reduce-scatter.5.cloned.1.call-start
  286.6 0.0 copy-done.8
  286.6 0.6 reduce_sum.18
  287.9 69.8 %all-to-all-done.3 = f32[3,256,8,128]{3,2,0,1:T(8,128)S(1)} async-done(((f32[3,256,8,128]{3,2,0,1:T(8,128)}), f32[3,256,8,128]{3,2,0,1:T(8,128)S(1)}, u32[]{:S(2)}, u32[]{:S(2)}) %all-to-all-start.3) | async-done | bytes 3145760 | tf_op jit(solution)/shard_map/all_to_all | solution.py:50
  357.6 0.0 copy-start.2
  357.6 0.2 copy.108
  357.9 0.0 copy-start.7
  357.9 0.5 multiply_reduce_fusion
  358.4 1.5 copy-done.7
  359.9 0.0 copy-start.5
  359.9 1.3 fusion.14
  361.2 0.0 copy-done.2
  361.2 2.9 fusion
  364.1 0.0 copy-done.5
  364.1 2.9 convolution_bitcast_fusion
  367.0 1.8 copy.114
  368.8 78.1 %all_to_all.132 = f32[3,16,128,128]{3,1,0,2:T(8,128)S(1)} all-to-all(f32[3,16,128,128]{3,1,0,2:T(8,128)S(1)} %copy.114), channel_id=1, replica_groups=mesh['grp'=16,'slab'=16] {'slab'}, dimensions={2} | all-to-all | bytes 6291456 | tf_op jit(solution)/shard_map/all_to_all | solution.py:47
  446.9 0.4 copy.115
  447.3 2.9 convolution_bitcast_fusion.2
  450.2 1.8 copy.116
  452.1 78.3 %all_to_all.133 = f32[3,256,8,128]{3,2,0,1:T(8,128)S(1)} all-to-all(f32[3,256,8,128]{3,2,0,1:T(8,128)S(1)} %copy.116), channel_id=1, replica_groups=mesh['grp'=16,'slab'=16] {'slab'}, dimensions={1} | all-to-all | bytes 6291456 | tf_op jit(solution)/shard_map/all_to_all | solution.py:50
  530.3 0.0 copy-start.4
  530.3 0.5 copy.117
  530.9 1.3 copy-done.4
  532.2 0.4 bitcast_divide_fusion
  532.6 78.1 %all_to_all.134 = f32[3,16,128,128]{3,1,0,2:T(8,128)S(1)} all-to-all(f32[3,16,128,128]{3,1,0,2:T(8,128)S(1)} %bitcast_divide_fusion), channel_id=1, replica_groups=mesh['grp'=16,'slab'=16] {'slab'}, dimensions={2} | all-to-all | bytes 6291456 | tf_op jit(solution)/shard_map/all_to_all | solution.py:61
  610.7 1.4 copy.118
  612.1 0.2 copy.128
  612.4 2.2 copy.144
  614.6 0.0 reduce-scatter.5.cloned.1.call-update
  614.6 0.0 copy-start.1
  614.6 1.5 copy_bitcast_fusion.1
  616.2 4.0 bitcast_divide_fusion.3
  620.1 56.7 %reduce-scatter.5.cloned.1.call-done = f32[16,3072]{1,0:T(8,128)} async-done(((f32[256,3072]{1,0:T(8,128)}), f32[16,3072]{1,0:T(8,128)}) %reduce-scatter.5.cloned.1.call-update) | async-done | bytes 196624
  676.9 1.0 copy.131
  677.8 0.7 copy.129
  678.5 0.0 copy-done.1
  (1 shorter events, 0.0 us)
Async XLA Ops:
  7.2 1.9 copy-start
  183.6 1.4 copy-start.6
  185.0 1.7 copy-start.3
  279.8 6.7 copy-start.8
  279.8 77.8 %all-to-all-start.3 = ((f32[3,256,8,128]{3,2,0,1:T(8,128)}), f32[3,256,8,128]{3,2,0,1:T(8,128)S(1)}, u32[]{:S(2)}, u32[]{:S(2)}) async-start(f32[3,256,8,128]{3,2,0,1:T(8,128)} %copy.107), calls=%async_computation.3 | async-start | bytes 6291456 | tf_op jit(solution)/shard_map/all_to_all | solution.py:50
  286.5 390.3 %reduce-scatter.5.cloned.1.call-start = ((), (), s32[]{:S(2)}) async-start(), calls=%async_computation.8 | async-start | bytes 3342336
  357.6 3.5 copy-start.2
  357.9 2.0 copy-start.7
  359.9 4.3 copy-start.5
  530.3 1.9 copy-start.4
  614.6 63.9 %copy-start.1 = (f32[1,3,16,128,128]{4,3,2,1,0:T(8,128)S(1)}, f32[1,3,16,128,128]{4,3,2,1,0:T(8,128)}, u32[]{:S(2)}) copy-start(f32[1,3,16,128,128]{4,3,2,1,0:T(8,128)} %param.5) | copy-start | bytes 9437188
Sparse Core Ops, SparseCore 0:
  614.7 62.0 reduce-scatter.4
where the time goes:
time: 696 us; the launch traced here: 686 us
  blocking collectives  474 us (68%)
  waiting for transfers between devices  127 us (18%)
  local copies, waits for them, and re-layouts  28.3 us (4%)
  matrix products  26.6 us (4%)
  between operations  15.1 us (2%)
  other arithmetic  7.92 us (1%)
    all_to_all x3, blocking collectives, stacked_entries(): lax.all_to_all(values, 'slab', split_axis=2, concat_axis=1, tiled=True)  239 us
    all_to_all x2, blocking collectives, reverse_lines(): lax.all_to_all(values, 'slab', split_axis=1, concat_axis=2, tiled=True)  157 us
    all_to_all x1, blocking collectives, local(): lax.all_to_all(gradient_planes, 'slab', split_axis=2, concat_axis=1, tile...  78.1 us
    all_to_all x1, waiting for transfers between devices, reverse_lines(): lax.all_to_all(values, 'slab', split_axis=1, concat_axis=2, tiled=True)  69.8 us
    unnamed x2, waiting for transfers between devices  56.7 us
  transfers between devices with their start and end apart: 2, of which 2 were waited for; matrix products, arithmetic and copies ran while one was open for 1% of the time, Pallas kernels for 0%

commit v1 on v0

v1 whole, which is shorter than its diff:
```python
import math

import jax
import jax.numpy as jnp
import ml_dtypes
import numpy as np
from jax import lax
from jax.experimental import pallas as pl
from jax.experimental.pallas import tpu as pltpu
from jax.sharding import PartitionSpec as P

REACH = 4
SHARPNESS = 3.0
ATOMS = 3
ROWS = 16
NY = 128
NZ = 128
HALF = 8
MESH = pl.DeviceIdType.MESH
f32 = jnp.float32
bf16 = jnp.bfloat16

TAPS = [math.exp(-SHARPNESS * (d / REACH) ** 2) / (REACH * math.sqrt(math.pi / SHARPNESS)) for d in range(REACH + 1)]

V_LOW, V_HIGH = math.log(0.0295), math.log(34.6)
F_LOW, F_HIGH = math.log(8.0e-4), math.log(5.2e3)


def code_of(low, high):
    scale = 65532.0 / (high - low)
    return scale, -32766.0 - low * scale


V_CODE = code_of(V_LOW, V_HIGH)
F_CODE = code_of(F_LOW, F_HIGH)


def encode(values, code):
    scale, shift = code
    return jnp.floor(jnp.log(values) * scale + (shift + 0.5)).astype(jnp.int32).astype(jnp.int16)


def decode(codes, code):
    scale, shift = code
    return jnp.exp(codes.astype(jnp.int32).astype(f32) * (1.0 / scale) - shift / scale)


def band(n):
    i = np.arange(n)
    offset = np.abs(i[:, None] - i[None, :])
    taps = np.array(TAPS, np.float32)
    return np.where(offset <= REACH, taps[np.minimum(offset, REACH)], np.float32(0))


def band_parts(n):
    g = band(n)
    high = g.astype(ml_dtypes.bfloat16)
    low = (g - high.astype(np.float32)).astype(ml_dtypes.bfloat16)
    return high, low


def matrices():
    high, low = band_parts(NZ)
    zero = np.zeros_like(low)
    along_z = np.block([[high, low], [high, zero]])
    high, low = band_parts(NY)
    zero = np.zeros_like(low)
    along_y = np.block([[high, high], [low, zero]])
    return along_z.astype(ml_dtypes.bfloat16), along_y.astype(ml_dtypes.bfloat16)


def parts(x):
    high = x.astype(bf16)
    return high, (x - high.astype(f32)).astype(bf16)


def kernel(
    v_hbm, b_hbm, p_hbm, tags, gz, gy,
    bary_hbm, scal_hbm, grad_hbm,
    vbuf, fbuf, rk, lk, bbuf, pbuf, bary, scal,
    s1, s2, s3, r1, r2, r3,
    gsend, crecv, ysum, yrecv, fsend, frecv, gout,
    in_sem, out_sem, h_send, h_recv, c_send, c_recv, y_send, y_recv, f_send, f_recv,
):
    g = lax.axis_index("grp")
    s = lax.axis_index("slab")
    y, lo, c = g // 4, (g // 2) % 2, g % 2
    left = (g, (s + 15) % 16)
    right = (g, (s + 1) % 16)
    twin = (y * 4 + lo * 2 + (1 - c), s)

    def across_y(d):
        return (((y + d) % 4) * 4 + lo * 2 + c, s)

    def owner(i):
        return (s, 4 * y + (1 - c) + 2 * i)

    def giver(l):
        return ((s // 4) * 4 + l * 2 + (1 - s % 2), g)

    v_in = [pltpu.make_async_copy(v_hbm.at[0, a], vbuf.at[a, pl.ds(REACH, ROWS)], in_sem.at[a]) for a in range(ATOMS)]
    p_in = pltpu.make_async_copy(p_hbm, pbuf, in_sem.at[3])
    b_in = pltpu.make_async_copy(b_hbm.at[0], bbuf, in_sem.at[4])
    for copy in v_in + [p_in, b_in]:
        copy.start()

    barrier = pltpu.get_barrier_semaphore()
    peers = [left, right, twin] + [across_y(d) for d in (1, 2, 3)] + [owner(0), owner(1), giver(0), giver(1)]
    for peer in peers:
        pl.semaphore_signal(barrier, inc=1, device_id=peer, device_id_type=MESH)
    pl.semaphore_wait(barrier, len(peers))

    has_left = (s > 0).astype(f32)
    has_right = (s < 15).astype(f32)

    def remote(src, dst, send, recv, device):
        return pltpu.make_async_remote_copy(src_ref=src, dst_ref=dst, send_sem=send, recv_sem=recv, device_id=device, device_id_type=MESH)

    def halos(stage, a):
        src, dst = ((s1, r1), (s2, r2), (s3, r3))[stage]
        return [
            remote(src.at[a, pl.ds(0, 4)], dst.at[a, 0], h_send.at[stage, a, 0], h_recv.at[stage, a, 0], right),
            remote(src.at[a, pl.ds(4, 4)], dst.at[a, 1], h_send.at[stage, a, 1], h_recv.at[stage, a, 1], left),
        ]

    def blur(buf, a, r):
        x = TAPS[0] * buf[a, r + REACH]
        for d in range(1, REACH + 1):
            x = x + TAPS[d] * (buf[a, r + REACH - d] + buf[a, r + REACH + d])
        high, low = parts(x)
        t = jnp.dot(jnp.concatenate([high, low], 1), gz[...], preferred_element_type=f32)
        high, low = parts(t[:, :NZ] + t[:, NZ:])
        t = jnp.dot(gy[...], jnp.concatenate([high, low], 0), preferred_element_type=f32)
        return t[:NY] + t[NY:]

    def row(part, i):
        return (4 + i) if part == 0 else (12 + i) % 16

    for a in range(ATOMS):
        v_in[a].wait()

        @pl.loop(0, HALF, unroll=2)
        def _(i):
            s1[a, i] = encode(vbuf[a, row(1, i) + REACH], V_CODE)

        for copy in halos(0, a):
            copy.start()

    p_in.wait()

    def first(a, part):
        @pl.loop(0, HALF, unroll=4)
        def _(i):
            r = row(part, i)
            k = 1.0 / blur(vbuf, a, r)
            rk[a, r] = k
            f = pbuf[a, r].astype(f32) * k
            fbuf[a, r + REACH] = f
            if part == 1:
                s2[a, i] = encode(f, F_CODE)

    def second(a, part):
        @pl.loop(0, HALF, unroll=4)
        def _(i):
            r = row(part, i)
            lk[a, r] = jnp.log(blur(fbuf, a, r))

    def land(stage, a, buf):
        for copy in halos(stage, a):
            copy.wait_recv()
        dst = (r1, r2, r3)[stage]

        def value(x):
            return x.astype(f32) if stage == 2 else decode(x, (V_CODE, F_CODE)[stage])

        @pl.loop(0, 4, unroll=2)
        def _(i):
            buf[a, i] = value(dst[a, 0, i]) * has_left
            buf[a, i + REACH + ROWS] = value(dst[a, 1, i]) * has_right

    for a in range(ATOMS):
        first(a, 0)
    for a in range(ATOMS):
        land(0, a, vbuf)
        first(a, 1)
        for copy in halos(1, a):
            copy.start()
        second(a, 0)

    total = jnp.zeros((8, NZ), f32)
    weights = []
    for a in range(ATOMS):
        weights.append(jnp.full((8, NZ), tags[0, a], jnp.int32).astype(f32))
        total = total + weights[a]
    blend = [(w / total)[:1] for w in weights]

    def middle(part):
        @pl.loop(0, HALF, unroll=2)
        def _(i):
            r = row(part, i)
            logs = [lk[a, r] for a in range(ATOMS)]
            mean = blend[0] * logs[0] + blend[1] * logs[1] + blend[2] * logs[2]
            center = jnp.exp(mean)
            bary[r] = center
            miss = center - bbuf[r]
            for a in range(ATOMS):
                ratio = jnp.exp(mean - logs[a])
                scal[a, r] = ratio
                pulled = blend[a] * miss * ratio
                vbuf[a, r + REACH] = pulled
                if part == 1:
                    s3[a, i] = pulled.astype(bf16)

    b_in.wait()
    land(1, 0, fbuf)
    second(0, 1)
    land(1, 1, fbuf)
    second(1, 1)
    middle(0)
    land(1, 2, fbuf)
    second(2, 1)
    middle(1)
    for a in range(ATOMS):
        for copy in halos(2, a):
            copy.start()
    results = [pltpu.make_async_copy(bary, bary_hbm.at[0], out_sem.at[0]), pltpu.make_async_copy(scal, scal_hbm.at[0], out_sem.at[1])]
    for copy in results:
        copy.start()

    def to_twin(a, part):
        return remote(gsend.at[a, part, c], crecv.at[a, part], c_send.at[a, part], c_recv.at[a, part], twin)

    def to_y(a, part, d):
        there = (y + d) % 4
        return remote(
            ysum.at[a, part, pl.ds(2 * there, 2)], yrecv.at[a, part, d - 1], y_send.at[a, part, d - 1], y_recv.at[a, part, d - 1], across_y(d)
        )

    def to_owner(a, part, i):
        return remote(fsend.at[a, part, i], frecv.at[a, part, lo], f_send.at[a, part, i], f_recv.at[a, part, lo], owner(i))

    def third(a, part):
        @pl.loop(0, HALF, unroll=4)
        def _(i):
            r = row(part, i)
            t = (blur(vbuf, a, r) * rk[a, r]).reshape(8, 2, 8, NZ)
            gsend[a, part, 0, :, i] = t[:, 0]
            gsend[a, part, 1, :, i] = t[:, 1]

        to_twin(a, part).start()

    def over_cores(a, part):
        to_twin(a, part).wait_recv()

        @pl.loop(0, 8, unroll=2)
        def _(j):
            ysum[a, part, j] = gsend[a, part, 1 - c, j] + crecv[a, part, j]

        for d in (2, 1, 3):
            to_y(a, part, d).start()

    def over_y(a, part):
        for d in (1, 3, 2):
            to_y(a, part, d).wait_recv()
        for i in range(2):
            t = ysum[a, part, 2 * y + i]
            for d in range(3):
                t = t + yrecv[a, part, d, i]
            fsend[a, part, i] = t
            to_owner(a, part, i).start()

    for a in range(ATOMS):
        third(a, 0)
    for a in range(ATOMS):
        over_cores(a, 0)
    land(2, 0, vbuf)
    third(0, 1)
    for a in range(ATOMS):
        over_y(a, 0)
    over_cores(0, 1)
    land(2, 1, vbuf)
    third(1, 1)
    over_y(0, 1)
    over_cores(1, 1)
    land(2, 2, vbuf)
    third(2, 1)
    over_y(1, 1)
    over_cores(2, 1)
    over_y(2, 1)

    for a in range(ATOMS):
        for part in range(2):
            for l in range(2):
                remote(fsend.at[a, part, 0], frecv.at[a, part, l], f_send.at[a, part, 0], f_recv.at[a, part, l], owner(0)).wait_recv()
            t = frecv[a, part, 0] + frecv[a, part, 1]
            if part == 0:
                gout[a, pl.ds(4, 8)] = t
            else:
                gout[a, pl.ds(12, 4)] = t[:4]
                gout[a, pl.ds(0, 4)] = t[4:]
    last = pltpu.make_async_copy(gout, grad_hbm, out_sem.at[2])
    last.start()

    for a in range(ATOMS):
        for stage in range(3):
            for copy in halos(stage, a):
                copy.wait_send()
        for part in range(2):
            to_twin(a, part).wait_send()
            for d in (1, 2, 3):
                to_y(a, part, d).wait_send()
            for i in range(2):
                to_owner(a, part, i).wait_send()
    for copy in results:
        copy.wait()
    last.wait()


def local(basis_atom_masses, right_dual_factors, observed_mass_snapshot, mixing_coefficient_tags):
    gz, gy = matrices()
    plane = (NY, NZ)
    vmem = pltpu.VMEM
    dma = pltpu.SemaphoreType.DMA
    anywhere = pl.BlockSpec(memory_space=pl.ANY)
    return pl.pallas_call(
        kernel,
        out_shape=(
            jax.ShapeDtypeStruct((1, ROWS) + plane, f32),
            jax.ShapeDtypeStruct((1, ATOMS, ROWS) + plane, f32),
            jax.ShapeDtypeStruct((ATOMS, ROWS, 8, NZ), f32),
        ),
        in_specs=[
            anywhere,
            anywhere,
            anywhere,
            pl.BlockSpec(memory_space=pltpu.SMEM),
            pl.BlockSpec(memory_space=vmem),
            pl.BlockSpec(memory_space=vmem),
        ],
        out_specs=(anywhere, anywhere, anywhere),
        scratch_shapes=[
            vmem((ATOMS, ROWS + 2 * REACH) + plane, f32),
            vmem((ATOMS, ROWS + 2 * REACH) + plane, f32),
            vmem((ATOMS, ROWS) + plane, f32),
            vmem((ATOMS, ROWS) + plane, f32),
            vmem((ROWS,) + plane, f32),
            vmem((ATOMS, ROWS) + plane, bf16),
            vmem((ROWS,) + plane, f32),
            vmem((ATOMS, ROWS) + plane, f32),
            vmem((ATOMS, HALF) + plane, jnp.int16),
            vmem((ATOMS, HALF) + plane, jnp.int16),
            vmem((ATOMS, HALF) + plane, bf16),
            vmem((ATOMS, 2, 4) + plane, jnp.int16),
            vmem((ATOMS, 2, 4) + plane, jnp.int16),
            vmem((ATOMS, 2, 4) + plane, bf16),
            vmem((ATOMS, 2, 2, 8, HALF, 8, NZ), f32),
            vmem((ATOMS, 2, 8, HALF, 8, NZ), f32),
            vmem((ATOMS, 2, 8, HALF, 8, NZ), f32),
            vmem((ATOMS, 2, 3, 2, HALF, 8, NZ), f32),
            vmem((ATOMS, 2, 2, HALF, 8, NZ), f32),
            vmem((ATOMS, 2, 2, HALF, 8, NZ), f32),
            vmem((ATOMS, ROWS, 8, NZ), f32),
            dma((5,)),
            dma((3,)),
            dma((3, ATOMS, 2)),
            dma((3, ATOMS, 2)),
            dma((ATOMS, 2)),
            dma((ATOMS, 2)),
            dma((ATOMS, 2, 3)),
            dma((ATOMS, 2, 3)),
            dma((ATOMS, 2, 2)),
            dma((ATOMS, 2, 2)),
        ],
        compiler_params=pltpu.CompilerParams(collective_id=0, has_side_effects=True, vmem_limit_bytes=60 * 2**20),
        name="sinkhorn_step",
    )(right_dual_factors, observed_mass_snapshot, basis_atom_masses, mixing_coefficient_tags, gz, gy)


def solution(mesh):
    placed = (
        P(None, "slab", None, None),
        P("grp", None, "slab", None, None),
        P("grp", "slab", None, None),
        P("grp", None),
    )
    return jax.shard_map(
        local,
        mesh=mesh,
        in_specs=placed,
        out_specs=(
            P("grp", "slab", None, None),
            P("grp", None, "slab", None, None),
            P(None, "grp", "slab", None),
        ),
        check_vma=False,
    )
```

time: 696 us -> 105 us (0.15)
  the two profiles are of different devices: /device:TPU:30 before, /device:TPU:22 now
where the time goes in v1:
time: 105 us
  Pallas kernels  97.6 us (93%)
  local copies, waits for them, and re-layouts  6.92 us (7%)
    pallas_call x1, Pallas kernels, local(): pl.pallas_call(kernel, out_shape=(jax.ShapeDtypeStruct((1, ROWS) + plane,...  97.6 us
    unnamed x5, local copies, waits for them, and re-layouts  6.92 us

profile of v1, /device:TPU:22, one launch (start us, length us, event | category | flops | bytes accessed | tf_op | source)
XLA Modules:
  0.0 105.2 jit_solution(4451563244142094596)
XLA Ops:
  0.6 97.6 %sinkhorn_step.1 = (f32[1,16,128,128]{3,2,1,0:T(8,128)}, f32[1,3,16,128,128]{4,3,2,1,0:T(8,128)}, f32[3,16,8,128]{3,2,1,0:T(8,128)}) custom-call(f32[1,3,16,128,128]{4,3,2,1,0:T(8,128)} %v_hbm.1, f32[1,16,128,128]{3,2,1,0:T(8,128)} %b_hbm.1, bf16[3,16,128,128]{3,2,1,0:T(8,128)(2,1)} %p_hbm.1, s32[1,3]{1,0:T(1,128)} %tags.1, ...), custom_call_target="tpu_custom_call" | custom-call | tf_op jit(solution)/shard_map/sinkhorn_step/pallas_call | solution.py:325
  98.3 2.3 %copy.12 = f32[1,16,128,128]{3,2,1,0:T(8,128)} copy(f32[1,16,128,128]{3,2,1,0:T(8,128)} %get-tuple-element.6) | data formatting | bytes 2097152
  100.6 0.0 copy-start
  100.6 3.9 %copy.13 = f32[1,3,16,128,128]{4,3,2,1,0:T(8,128)} copy(f32[1,3,16,128,128]{4,3,2,1,0:T(8,128)} %get-tuple-element.7) | data formatting | bytes 6291456
  104.5 0.0 copy-done
  104.5 0.7 copy.14
Async XLA Ops:
  100.6 4.0 %copy-start = (f32[3,16,8,128]{3,2,1,0:T(8,128)S(1)}, f32[3,16,8,128]{3,2,1,0:T(8,128)}, u32[]{:S(2)}) copy-start(f32[3,16,8,128]{3,2,1,0:T(8,128)} %get-tuple-element.8) | copy-start | bytes 589828

commit v2 on v1

--- a/solution.py
+++ b/solution.py
@@ -19,6 +19,9 @@
 MESH = pl.DeviceIdType.MESH
 f32 = jnp.float32
 bf16 = jnp.bfloat16
+LN2 = math.log(2.0)
+CODE_TOP = 32760.0
+VMEM_LIMIT = 61184 * 2**10
 
 TAPS = [math.exp(-SHARPNESS * (d / REACH) ** 2) / (REACH * math.sqrt(math.pi / SHARPNESS)) for d in range(REACH + 1)]
 
@@ -45,28 +48,16 @@
     return jnp.exp(codes.astype(jnp.int32).astype(f32) * (1.0 / scale) - shift / scale)
 
 
-def band(n):
-    i = np.arange(n)
-    offset = np.abs(i[:, None] - i[None, :])
-    taps = np.array(TAPS, np.float32)
-    return np.where(offset <= REACH, taps[np.minimum(offset, REACH)], np.float32(0))
-
-
-def band_parts(n):
-    g = band(n)
-    high = g.astype(ml_dtypes.bfloat16)
-    low = (g - high.astype(np.float32)).astype(ml_dtypes.bfloat16)
-    return high, low
-
-
-def matrices():
-    high, low = band_parts(NZ)
-    zero = np.zeros_like(low)
-    along_z = np.block([[high, low], [high, zero]])
-    high, low = band_parts(NY)
-    zero = np.zeros_like(low)
-    along_y = np.block([[high, high], [low, zero]])
-    return along_z.astype(ml_dtypes.bfloat16), along_y.astype(ml_dtypes.bfloat16)
+HIGH = [float(np.float32(t).astype(ml_dtypes.bfloat16)) for t in TAPS]
+LOW = [float((np.float32(t) - np.float32(h)).astype(ml_dtypes.bfloat16)) for t, h in zip(TAPS, HIGH)]
+
+
+def band(taps, n):
+    offset = jnp.abs(lax.broadcasted_iota(jnp.int32, (n, n), 0) - lax.broadcasted_iota(jnp.int32, (n, n), 1))
+    g = jnp.zeros((n, n), f32)
+    for d, tap in enumerate(taps):
+        g = jnp.where(offset == d, tap, g)
+    return g.astype(bf16)
 
 
 def parts(x):
@@ -75,12 +66,12 @@
 
 
 def kernel(
-    v_hbm, b_hbm, p_hbm, tags, gz, gy,
-    bary_hbm, scal_hbm, grad_hbm,
-    vbuf, fbuf, rk, lk, bbuf, pbuf, bary, scal,
+    v_hbm, b_hbm, p_hbm, tags,
+    bary, scal, gout,
+    gz, gy, vbuf, fbuf, rk, lk, bbuf, pbuf,
     s1, s2, s3, r1, r2, r3,
-    gsend, crecv, ysum, yrecv, fsend, frecv, gout,
-    in_sem, out_sem, h_send, h_recv, c_send, c_recv, y_send, y_recv, f_send, f_recv,
+    gsend, crecv, ysum, ycode, yrecv, fsize, fsend0, fsend1, frecv0, frecv1,
+    in_sem, h_send, h_recv, c_send, c_recv, y_send, y_recv, f_send, f_recv,
 ):
     g = lax.axis_index("grp")
     s = lax.axis_index("slab")
@@ -92,11 +83,20 @@
     def across_y(d):
         return (((y + d) % 4) * 4 + lo * 2 + c, s)
 
+    z = s // 2
+    pair = (y + 2 * c) % 4
+
+    def ahead(k, i):
+        return (z + k + 4 * i) % 8
+
     def owner(i):
-        return (s, 4 * y + (1 - c) + 2 * i)
+        return (s, 2 * ahead(pair, i) + 1 - c)
+
+    giver_core = 1 - s % 2
+    giver_y = ((s // 2 - g // 2 + 8) % 8 + 4 - 2 * giver_core) % 4
 
     def giver(l):
-        return ((s // 4) * 4 + l * 2 + (1 - s % 2), g)
+        return (giver_y * 4 + l * 2 + giver_core, g)
 
     v_in = [pltpu.make_async_copy(v_hbm.at[0, a], vbuf.at[a, pl.ds(REACH, ROWS)], in_sem.at[a]) for a in range(ATOMS)]
     p_in = pltpu.make_async_copy(p_hbm, pbuf, in_sem.at[3])
@@ -108,7 +108,10 @@
     peers = [left, right, twin] + [across_y(d) for d in (1, 2, 3)] + [owner(0), owner(1), giver(0), giver(1)]
     for peer in peers:
         pl.semaphore_signal(barrier, inc=1, device_id=peer, device_id_type=MESH)
-    pl.semaphore_wait(barrier, len(peers))
+
+    high, low, zero = band(HIGH, NZ), band(LOW, NZ), jnp.zeros((NZ, NZ), bf16)
+    gz[...] = jnp.concatenate([jnp.concatenate([high, low], 1), jnp.concatenate([high, zero], 1)], 0)
+    gy[...] = jnp.concatenate([jnp.concatenate([high, high], 1), jnp.concatenate([low, zero], 1)], 0)
 
     has_left = (s > 0).astype(f32)
     has_right = (s < 15).astype(f32)
@@ -143,6 +146,8 @@
         def _(i):
             s1[a, i] = encode(vbuf[a, row(1, i) + REACH], V_CODE)
 
+        if a == 0:
+            pl.semaphore_wait(barrier, len(peers))
         for copy in halos(0, a):
             copy.start()
 
@@ -201,11 +206,11 @@
             logs = [lk[a, r] for a in range(ATOMS)]
             mean = blend[0] * logs[0] + blend[1] * logs[1] + blend[2] * logs[2]
             center = jnp.exp(mean)
-            bary[r] = center
+            bary[0, r] = center
             miss = center - bbuf[r]
             for a in range(ATOMS):
                 ratio = jnp.exp(mean - logs[a])
-                scal[a, r] = ratio
+                scal[0, a, r] = ratio
                 pulled = blend[a] * miss * ratio
                 vbuf[a, r + REACH] = pulled
                 if part == 1:
@@ -223,21 +228,43 @@
     for a in range(ATOMS):
         for copy in halos(2, a):
             copy.start()
-    results = [pltpu.make_async_copy(bary, bary_hbm.at[0], out_sem.at[0]), pltpu.make_async_copy(scal, scal_hbm.at[0], out_sem.at[1])]
-    for copy in results:
-        copy.start()
 
     def to_twin(a, part):
         return remote(gsend.at[a, part, c], crecv.at[a, part], c_send.at[a, part], c_recv.at[a, part], twin)
 
     def to_y(a, part, d):
-        there = (y + d) % 4
         return remote(
-            ysum.at[a, part, pl.ds(2 * there, 2)], yrecv.at[a, part, d - 1], y_send.at[a, part, d - 1], y_recv.at[a, part, d - 1], across_y(d)
+            ycode.at[a, part, (pair + d) % 4], yrecv.at[a, part, d - 1], y_send.at[a, part, d - 1], y_recv.at[a, part, d - 1], across_y(d)
         )
 
     def to_owner(a, part, i):
-        return remote(fsend.at[a, part, i], frecv.at[a, part, lo], f_send.at[a, part, i], f_recv.at[a, part, lo], owner(i))
+        if part == 0:
+            src, dst, n = fsend0.at[i], frecv0.at[lo], 0
+        else:
+            src, dst, n = fsend1.at[a, i], frecv1.at[a, lo], 1 + a
+        return remote(src, dst, f_send.at[n, i], f_recv.at[n, lo], owner(i))
+
+    def from_giver(a, part, l):
+        if part == 0:
+            src, dst, n = fsend0.at[0], frecv0.at[l], 0
+        else:
+            src, dst, n = fsend1.at[a, 0], frecv1.at[a, l], 1 + a
+        return remote(src, dst, f_send.at[n, 0], f_recv.at[n, l], owner(0))
+
+    def pack(t):
+        top = jnp.maximum(jnp.max(jnp.abs(t), axis=0), 1e-30)
+        size = jnp.ceil(jnp.log(top) * (16.0 / LN2))
+        code = jnp.floor(t * (CODE_TOP * jnp.exp(size * (-LN2 / 16.0)))[None] + 0.5)
+        return code.reshape(64, NZ).astype(jnp.int32).astype(jnp.int16), size
+
+    def narrow(size):
+        return size.astype(jnp.int32).astype(jnp.int16)
+
+    def units(size):
+        return jnp.exp(size.astype(jnp.int32).astype(f32) * (LN2 / 16.0)) * (1.0 / CODE_TOP)
+
+    def unpack(code, unit):
+        return code.astype(jnp.int32).astype(f32).reshape(HALF, 8, NZ) * unit[None]
 
     def third(a, part):
         @pl.loop(0, HALF, unroll=4)
@@ -252,9 +279,16 @@
     def over_cores(a, part):
         to_twin(a, part).wait_recv()
 
-        @pl.loop(0, 8, unroll=2)
-        def _(j):
-            ysum[a, part, j] = gsend[a, part, 1 - c, j] + crecv[a, part, j]
+        @pl.loop(0, 4)
+        def _(k):
+            sizes = []
+            for i in range(2):
+                j = ahead(k, i)
+                t = gsend[a, part, 1 - c, j] + crecv[a, part, j]
+                ysum[a, part, k, i] = t
+                ycode[a, part, k, pl.ds(64 * i, 64)], size = pack(t)
+                sizes.append(size)
+            ycode[a, part, k, pl.ds(128, 16)] = narrow(jnp.concatenate(sizes, 0))
 
         for d in (2, 1, 3):
             to_y(a, part, d).start()
@@ -262,12 +296,23 @@
     def over_y(a, part):
         for d in (1, 3, 2):
             to_y(a, part, d).wait_recv()
+        scales = [units(yrecv[a, part, d, pl.ds(128, 16)]) for d in range(3)]
         for i in range(2):
-            t = ysum[a, part, 2 * y + i]
+            t = ysum[a, part, pair, i]
             for d in range(3):
-                t = t + yrecv[a, part, d, i]
-            fsend[a, part, i] = t
-            to_owner(a, part, i).start()
+                t = t + unpack(yrecv[a, part, d, pl.ds(64 * i, 64)], scales[d][8 * i : 8 * i + 8])
+            code, size = pack(t)
+            if part == 0:
+                fsend0[i, pl.ds(64 * a, 64)] = code
+                fsize[a, i] = size
+                if a == ATOMS - 1:
+                    sizes = jnp.concatenate([fsize[0, i], fsize[1, i], size, size], 0)
+                    fsend0[i, pl.ds(192, 32)] = narrow(sizes)
+                    to_owner(a, part, i).start()
+            else:
+                fsend1[a, i, pl.ds(0, 64)] = code
+                fsend1[a, i, pl.ds(64, 16)] = narrow(jnp.concatenate([size, size], 0))
+                to_owner(a, part, i).start()
 
     for a in range(ATOMS):
         third(a, 0)
@@ -288,18 +333,19 @@
     over_cores(2, 1)
     over_y(2, 1)
 
-    for a in range(ATOMS):
-        for part in range(2):
-            for l in range(2):
-                remote(fsend.at[a, part, 0], frecv.at[a, part, l], f_send.at[a, part, 0], f_recv.at[a, part, l], owner(0)).wait_recv()
-            t = frecv[a, part, 0] + frecv[a, part, 1]
-            if part == 0:
-                gout[a, pl.ds(4, 8)] = t
-            else:
-                gout[a, pl.ds(12, 4)] = t[:4]
-                gout[a, pl.ds(0, 4)] = t[4:]
-    last = pltpu.make_async_copy(gout, grad_hbm, out_sem.at[2])
-    last.start()
+    for l in range(2):
+        from_giver(0, 0, l).wait_recv()
+    scales = [units(frecv0[l, pl.ds(192, 32)]) for l in range(2)]
+    for a in range(ATOMS):
+        t = [unpack(frecv0[l, pl.ds(64 * a, 64)], scales[l][8 * a : 8 * a + 8]) for l in range(2)]
+        gout[a, pl.ds(4, 8)] = t[0] + t[1]
+    for a in range(ATOMS):
+        for l in range(2):
+            from_giver(a, 1, l).wait_recv()
+        t = [unpack(frecv1[a, l, pl.ds(0, 64)], units(frecv1[a, l, pl.ds(64, 16)])[:8]) for l in range(2)]
+        t = t[0] + t[1]
+        gout[a, pl.ds(12, 4)] = t[:4]
+        gout[a, pl.ds(0, 4)] = t[4:]
 
     for a in range(ATOMS):
         for stage in range(3):
@@ -309,44 +355,38 @@
             to_twin(a, part).wait_send()
             for d in (1, 2, 3):
                 to_y(a, part, d).wait_send()
-            for i in range(2):
+            for i in range(2 if part or a == 0 else 0):
                 to_owner(a, part, i).wait_send()
-    for copy in results:
-        copy.wait()
-    last.wait()
 
 
 def local(basis_atom_masses, right_dual_factors, observed_mass_snapshot, mixing_coefficient_tags):
-    gz, gy = matrices()
     plane = (NY, NZ)
     vmem = pltpu.VMEM
     dma = pltpu.SemaphoreType.DMA
-    anywhere = pl.BlockSpec(memory_space=pl.ANY)
+    outside = pl.BlockSpec(memory_space=pltpu.HBM)
     return pl.pallas_call(
         kernel,
         out_shape=(
-            jax.ShapeDtypeStruct((1, ROWS) + plane, f32),
-            jax.ShapeDtypeStruct((1, ATOMS, ROWS) + plane, f32),
-            jax.ShapeDtypeStruct((ATOMS, ROWS, 8, NZ), f32),
+            vmem((1, ROWS) + plane, f32),
+            vmem((1, ATOMS, ROWS) + plane, f32),
+            vmem((ATOMS, ROWS, 8, NZ), f32),
         ),
         in_specs=[
-            anywhere,
-            anywhere,
-            anywhere,
+            outside,
+            outside,
+            outside,
             pl.BlockSpec(memory_space=pltpu.SMEM),
-            pl.BlockSpec(memory_space=vmem),
-            pl.BlockSpec(memory_space=vmem),
         ],
-        out_specs=(anywhere, anywhere, anywhere),
+        out_specs=(pl.BlockSpec(memory_space=vmem),) * 3,
         scratch_shapes=[
+            vmem((2 * NZ, 2 * NZ), bf16),
+            vmem((2 * NY, 2 * NY), bf16),
             vmem((ATOMS, ROWS + 2 * REACH) + plane, f32),
             vmem((ATOMS, ROWS + 2 * REACH) + plane, f32),
             vmem((ATOMS, ROWS) + plane, f32),
             vmem((ATOMS, ROWS) + plane, f32),
             vmem((ROWS,) + plane, f32),
             vmem((ATOMS, ROWS) + plane, bf16),
-            vmem((ROWS,) + plane, f32),
-            vmem((ATOMS, ROWS) + plane, f32),
             vmem((ATOMS, HALF) + plane, jnp.int16),
             vmem((ATOMS, HALF) + plane, jnp.int16),
             vmem((ATOMS, HALF) + plane, bf16),
@@ -355,25 +395,27 @@
             vmem((ATOMS, 2, 4) + plane, bf16),
             vmem((ATOMS, 2, 2, 8, HALF, 8, NZ), f32),
             vmem((ATOMS, 2, 8, HALF, 8, NZ), f32),
-            vmem((ATOMS, 2, 8, HALF, 8, NZ), f32),
-            vmem((ATOMS, 2, 3, 2, HALF, 8, NZ), f32),
-            vmem((ATOMS, 2, 2, HALF, 8, NZ), f32),
-            vmem((ATOMS, 2, 2, HALF, 8, NZ), f32),
-            vmem((ATOMS, ROWS, 8, NZ), f32),
+            vmem((ATOMS, 2, 4, 2, HALF, 8, NZ), f32),
+            vmem((ATOMS, 2, 4, 144, NZ), jnp.int16),
+            vmem((ATOMS, 2, 3, 144, NZ), jnp.int16),
+            vmem((ATOMS, 2, 8, NZ), f32),
+            vmem((2, 224, NZ), jnp.int16),
+            vmem((ATOMS, 2, 80, NZ), jnp.int16),
+            vmem((2, 224, NZ), jnp.int16),
+            vmem((ATOMS, 2, 80, NZ), jnp.int16),
             dma((5,)),
-            dma((3,)),
             dma((3, ATOMS, 2)),
             dma((3, ATOMS, 2)),
             dma((ATOMS, 2)),
             dma((ATOMS, 2)),
             dma((ATOMS, 2, 3)),
             dma((ATOMS, 2, 3)),
-            dma((ATOMS, 2, 2)),
-            dma((ATOMS, 2, 2)),
+            dma((1 + ATOMS, 2)),
+            dma((1 + ATOMS, 2)),
         ],
-        compiler_params=pltpu.CompilerParams(collective_id=0, has_side_effects=True, vmem_limit_bytes=60 * 2**20),
+        compiler_params=pltpu.CompilerParams(collective_id=0, has_side_effects=True, vmem_limit_bytes=VMEM_LIMIT),
         name="sinkhorn_step",
-    )(right_dual_factors, observed_mass_snapshot, basis_atom_masses, mixing_coefficient_tags, gz, gy)
+    )(right_dual_factors, observed_mass_snapshot, basis_atom_masses, mixing_coefficient_tags)
 
 
 def solution(mesh):

time: 105 us -> 89.5 us (0.85)
  the two profiles are of different devices: /device:TPU:22 before, /device:TPU:30 now
where the time goes in v2:
time: 89.5 us; the launch traced here: 88 us
  Pallas kernels  84.1 us (94%)
  local copies, waits for them, and re-layouts  3.31 us (4%)
    pallas_call x1, Pallas kernels, local(): pl.pallas_call(kernel, out_shape=(vmem((1, ROWS) + plane, f32), vmem((1,...  84.1 us
    unnamed x3, local copies, waits for them, and re-layouts  3.31 us

profile of v2, /device:TPU:30, one launch (start us, length us, event | category | flops | bytes accessed | tf_op | source)
XLA Modules:
  0.0 88.0 jit_solution(10399239688108473417)
XLA Ops:
  0.6 84.1 %sinkhorn_step.1 = (f32[1,16,128,128]{3,2,1,0:T(8,128)S(1)}, f32[1,3,16,128,128]{4,3,2,1,0:T(8,128)S(1)}, f32[3,16,8,128]{3,2,1,0:T(8,128)S(1)}) custom-call(f32[1,3,16,128,128]{4,3,2,1,0:T(8,128)} %v_hbm.1, f32[1,16,128,128]{3,2,1,0:T(8,128)} %b_hbm.1, bf16[3,16,128,128]{3,2,1,0:T(8,128)(2,1)} %p_hbm.1, s32[1,3]{1,0:T(1,128)} %tags.1), custom_call_target="tpu_custom_call" | custom-call | tf_op jit(solution)/shard_map/sinkhorn_step/pallas_call | solution.py:367
  84.7 1.0 %copy.10 = f32[1,16,128,128]{3,2,1,0:T(8,128)} copy(f32[1,16,128,128]{3,2,1,0:T(8,128)S(1)} %get-tuple-element.3) | data formatting | bytes 2097152
  85.7 0.7 copy.12
  86.4 1.7 %copy.11 = f32[1,3,16,128,128]{4,3,2,1,0:T(8,128)} copy(f32[1,3,16,128,128]{4,3,2,1,0:T(8,128)S(1)} %get-tuple-element.4) | data formatting | bytes 6291456

commit v3 on v2

--- a/solution.py
+++ b/solution.py
@@ -119,12 +119,14 @@
     def remote(src, dst, send, recv, device):
         return pltpu.make_async_remote_copy(src_ref=src, dst_ref=dst, send_sem=send, recv_sem=recv, device_id=device, device_id_type=MESH)
 
+    def halo(stage, a, q):
+        src, dst = ((s1, r1), (s2, r2), (s3, r3))[stage]
+        return remote(
+            src.at[a, pl.ds(4 * q, 4)], dst.at[a, q], h_send.at[stage, a, q], h_recv.at[stage, a, q], (right, left)[q]
+        )
+
     def halos(stage, a):
-        src, dst = ((s1, r1), (s2, r2), (s3, r3))[stage]
-        return [
-            remote(src.at[a, pl.ds(0, 4)], dst.at[a, 0], h_send.at[stage, a, 0], h_recv.at[stage, a, 0], right),
-            remote(src.at[a, pl.ds(4, 4)], dst.at[a, 1], h_send.at[stage, a, 1], h_recv.at[stage, a, 1], left),
-        ]
+        return [halo(stage, a, q) for q in range(2)]
 
     def blur(buf, a, r):
         x = TAPS[0] * buf[a, r + REACH]
@@ -153,8 +155,11 @@
 
     p_in.wait()
 
+    def span(side):
+        return (0, HALF) if side is None else (4 * side, 4 * side + 4)
+
     def first(a, part):
-        @pl.loop(0, HALF, unroll=4)
+        @pl.loop(0, HALF, unroll=8 if part else 4)
         def _(i):
             r = row(part, i)
             k = 1.0 / blur(vbuf, a, r)
@@ -164,24 +169,27 @@
             if part == 1:
                 s2[a, i] = encode(f, F_CODE)
 
-    def second(a, part):
-        @pl.loop(0, HALF, unroll=4)
+    def second(a, part, side=None):
+        @pl.loop(*span(side), unroll=8 if part and side is None else 4)
         def _(i):
             r = row(part, i)
             lk[a, r] = jnp.log(blur(fbuf, a, r))
 
-    def land(stage, a, buf):
-        for copy in halos(stage, a):
-            copy.wait_recv()
+    def land(stage, a, buf, side=None):
+        sides = (0, 1) if side is None else (side,)
+        for q in sides:
+            halo(stage, a, 1 - q).wait_recv()
         dst = (r1, r2, r3)[stage]
 
         def value(x):
             return x.astype(f32) if stage == 2 else decode(x, (V_CODE, F_CODE)[stage])
 
-        @pl.loop(0, 4, unroll=2)
-        def _(i):
-            buf[a, i] = value(dst[a, 0, i]) * has_left
-            buf[a, i + REACH + ROWS] = value(dst[a, 1, i]) * has_right
+        @pl.loop(0, 4, unroll=4)
+        def _(i):
+            if 1 in sides:
+                buf[a, i] = value(dst[a, 0, i]) * has_left
+            if 0 in sides:
+                buf[a, i + REACH + ROWS] = value(dst[a, 1, i]) * has_right
 
     for a in range(ATOMS):
         first(a, 0)
@@ -199,8 +207,8 @@
         total = total + weights[a]
     blend = [(w / total)[:1] for w in weights]
 
-    def middle(part):
-        @pl.loop(0, HALF, unroll=2)
+    def middle(part, side=None):
+        @pl.loop(*span(side), unroll=2)
         def _(i):
             r = row(part, i)
             logs = [lk[a, r] for a in range(ATOMS)]
@@ -222,12 +230,12 @@
     land(1, 1, fbuf)
     second(1, 1)
     middle(0)
-    land(1, 2, fbuf)
-    second(2, 1)
-    middle(1)
-    for a in range(ATOMS):
-        for copy in halos(2, a):
-            copy.start()
+    for side in range(2):
+        land(1, 2, fbuf, side)
+        second(2, 1, side)
+        middle(1, side)
+        for a in range(ATOMS):
+            halo(2, a, side).start()
 
     def to_twin(a, part):
         return remote(gsend.at[a, part, c], crecv.at[a, part], c_send.at[a, part], c_recv.at[a, part], twin)
@@ -267,7 +275,7 @@
         return code.astype(jnp.int32).astype(f32).reshape(HALF, 8, NZ) * unit[None]
 
     def third(a, part):
-        @pl.loop(0, HALF, unroll=4)
+        @pl.loop(0, HALF, unroll=8 if part else 4)
         def _(i):
             r = row(part, i)
             t = (blur(vbuf, a, r) * rk[a, r]).reshape(8, 2, 8, NZ)
@@ -279,7 +287,7 @@
     def over_cores(a, part):
         to_twin(a, part).wait_recv()
 
-        @pl.loop(0, 4)
+        @pl.loop(0, 4, unroll=4)
         def _(k):
             sizes = []
             for i in range(2):

time: 89.5 us -> 89.3 us (level); the launches traced: 88 us -> 89.2 us
  Pallas kernels: 84.1 us -> 85.3 us
    pallas_call x1, Pallas kernels: 84.1 us -> 85.3 us  [local(): pl.pallas_call(kernel, out_shape=(vmem((1, ROWS) + plane, f32), vmem((1,...]
where the time goes in v3:
time: 89.3 us; the launch traced here: 89.2 us
  Pallas kernels  85.3 us (96%)
  local copies, waits for them, and re-layouts  3.31 us (4%)
    pallas_call x1, Pallas kernels, local(): pl.pallas_call(kernel, out_shape=(vmem((1, ROWS) + plane, f32), vmem((1,...  85.3 us
    unnamed x3, local copies, waits for them, and re-layouts  3.31 us

profile of v3, /device:TPU:30, one launch (start us, length us, event | category | flops | bytes accessed | tf_op | source)
XLA Modules:
  0.0 89.2 jit_solution(17681592394025782853)
XLA Ops:
  0.6 85.3 %sinkhorn_step.1 = (f32[1,16,128,128]{3,2,1,0:T(8,128)S(1)}, f32[1,3,16,128,128]{4,3,2,1,0:T(8,128)S(1)}, f32[3,16,8,128]{3,2,1,0:T(8,128)S(1)}) custom-call(f32[1,3,16,128,128]{4,3,2,1,0:T(8,128)} %v_hbm.1, f32[1,16,128,128]{3,2,1,0:T(8,128)} %b_hbm.1, bf16[3,16,128,128]{3,2,1,0:T(8,128)(2,1)} %p_hbm.1, s32[1,3]{1,0:T(1,128)} %tags.1), custom_call_target="tpu_custom_call" | custom-call | tf_op jit(solution)/shard_map/sinkhorn_step/pallas_call | solution.py:375
  85.9 1.0 %copy.10 = f32[1,16,128,128]{3,2,1,0:T(8,128)} copy(f32[1,16,128,128]{3,2,1,0:T(8,128)S(1)} %get-tuple-element.3) | data formatting | bytes 2097152
  86.9 0.7 copy.12
  87.6 1.7 %copy.11 = f32[1,3,16,128,128]{4,3,2,1,0:T(8,128)} copy(f32[1,3,16,128,128]{4,3,2,1,0:T(8,128)S(1)} %get-tuple-element.4) | data formatting | bytes 6291456

commit v4 on v3

--- a/solution.py
+++ b/solution.py
@@ -225,11 +225,11 @@
                     s3[a, i] = pulled.astype(bf16)
 
     b_in.wait()
+    middle(0)
     land(1, 0, fbuf)
     second(0, 1)
     land(1, 1, fbuf)
     second(1, 1)
-    middle(0)
     for side in range(2):
         land(1, 2, fbuf, side)
         second(2, 1, side)
@@ -337,8 +337,8 @@
     over_cores(1, 1)
     land(2, 2, vbuf)
     third(2, 1)
+    over_cores(2, 1)
     over_y(1, 1)
-    over_cores(2, 1)
     over_y(2, 1)
 
     for l in range(2):

time: 89.3 us -> 86.8 us (0.972)
  Pallas kernels: 85.3 us -> 82.7 us
    pallas_call x1, Pallas kernels: 85.3 us -> 82.7 us  [local(): pl.pallas_call(kernel, out_shape=(vmem((1, ROWS) + plane, f32), vmem((1,...]
where the time goes in v4:
time: 86.8 us; the launch traced here: 86.7 us
  Pallas kernels  82.7 us (95%)
  local copies, waits for them, and re-layouts  3.31 us (4%)
    pallas_call x1, Pallas kernels, local(): pl.pallas_call(kernel, out_shape=(vmem((1, ROWS) + plane, f32), vmem((1,...  82.7 us
    unnamed x3, local copies, waits for them, and re-layouts  3.31 us

profile of v4, /device:TPU:30, one launch (start us, length us, event | category | flops | bytes accessed | tf_op | source)
XLA Modules:
  0.0 86.7 jit_solution(74285173364047312)
XLA Ops:
  0.6 82.7 %sinkhorn_step.1 = (f32[1,16,128,128]{3,2,1,0:T(8,128)S(1)}, f32[1,3,16,128,128]{4,3,2,1,0:T(8,128)S(1)}, f32[3,16,8,128]{3,2,1,0:T(8,128)S(1)}) custom-call(f32[1,3,16,128,128]{4,3,2,1,0:T(8,128)} %v_hbm.1, f32[1,16,128,128]{3,2,1,0:T(8,128)} %b_hbm.1, bf16[3,16,128,128]{3,2,1,0:T(8,128)(2,1)} %p_hbm.1, s32[1,3]{1,0:T(1,128)} %tags.1), custom_call_target="tpu_custom_call" | custom-call | tf_op jit(solution)/shard_map/sinkhorn_step/pallas_call | solution.py:375
  83.4 1.0 %copy.10 = f32[1,16,128,128]{3,2,1,0:T(8,128)} copy(f32[1,16,128,128]{3,2,1,0:T(8,128)S(1)} %get-tuple-element.3) | data formatting | bytes 2097152
  84.3 0.7 copy.12
  85.0 1.7 %copy.11 = f32[1,3,16,128,128]{4,3,2,1,0:T(8,128)} copy(f32[1,3,16,128,128]{4,3,2,1,0:T(8,128)S(1)} %get-tuple-element.4) | data formatting | bytes 6291456

commit v5 on v4

--- a/solution.py
+++ b/solution.py
@@ -333,8 +333,8 @@
     over_cores(0, 1)
     land(2, 1, vbuf)
     third(1, 1)
+    over_cores(1, 1)
     over_y(0, 1)
-    over_cores(1, 1)
     land(2, 2, vbuf)
     third(2, 1)
     over_cores(2, 1)

time: 86.8 us -> 86.9 us (level)
  no operation moved by 1% of the time
where the time goes in v5:
time: 86.9 us; the launch traced here: 86.3 us
  Pallas kernels  82.4 us (95%)
  local copies, waits for them, and re-layouts  3.31 us (4%)
    pallas_call x1, Pallas kernels, local(): pl.pallas_call(kernel, out_shape=(vmem((1, ROWS) + plane, f32), vmem((1,...  82.4 us
    unnamed x3, local copies, waits for them, and re-layouts  3.31 us

profile of v5, /device:TPU:30, one launch (start us, length us, event | category | flops | bytes accessed | tf_op | source)
XLA Modules:
  0.0 86.3 jit_solution(10919423394789960993)
XLA Ops:
  0.6 82.4 %sinkhorn_step.1 = (f32[1,16,128,128]{3,2,1,0:T(8,128)S(1)}, f32[1,3,16,128,128]{4,3,2,1,0:T(8,128)S(1)}, f32[3,16,8,128]{3,2,1,0:T(8,128)S(1)}) custom-call(f32[1,3,16,128,128]{4,3,2,1,0:T(8,128)} %v_hbm.1, f32[1,16,128,128]{3,2,1,0:T(8,128)} %b_hbm.1, bf16[3,16,128,128]{3,2,1,0:T(8,128)(2,1)} %p_hbm.1, s32[1,3]{1,0:T(1,128)} %tags.1), custom_call_target="tpu_custom_call" | custom-call | tf_op jit(solution)/shard_map/sinkhorn_step/pallas_call | solution.py:375
  83.0 1.0 %copy.10 = f32[1,16,128,128]{3,2,1,0:T(8,128)} copy(f32[1,16,128,128]{3,2,1,0:T(8,128)S(1)} %get-tuple-element.3) | data formatting | bytes 2097152
  84.0 0.7 copy.12
  84.7 1.7 %copy.11 = f32[1,3,16,128,128]{4,3,2,1,0:T(8,128)} copy(f32[1,3,16,128,128]{4,3,2,1,0:T(8,128)S(1)} %get-tuple-element.4) | data formatting | bytes 6291456
